TPU v7x, 32 devices: a whole 2x2x4 slice. The times are simulated.
32 devices in a mesh: ctx: 8 (over z, x), head: 4 (over y, core).
Axes of the slice: x: 2, y: 2, z: 4, core: 2. Of those that a mesh axis runs over, the one named last changes fastest.
Arguments:
- query_rows: bfloat16 [4096, 5120], P(('ctx', 'head')), may hold values from -6 to 6
- key_rows: bfloat16 [4096, 1024], P(('ctx', 'head')), may hold values from -6 to 6
- value_rows: bfloat16 [4096, 1024], P(('ctx', 'head')), may hold values from -6 to 6
- attn_output: bfloat16 [4096, 5120], P(('ctx', 'head')), may hold values from -3 to 3
- out_grad: bfloat16 [4096, 5120], P(('ctx', 'head')), may hold values from -24 to 24
- log_norm: float32 [40, 4096], P('head', 'ctx'), may hold values from 5 to 7
- prefix_keys: bfloat16 [128, 1024], P('ctx', 'head'), may hold values from -6 to 6
- prefix_values: bfloat16 [128, 1024], P('ctx', 'head'), may hold values from -6 to 6
- response_blocks: int32 [16], replicated, may hold values from 1 to 16, as said below
- prompt_members: int32 [1, 16], replicated, may hold values from 0 to 15, as said below
Outputs:
- query_grad: bfloat16 [4096, 5120], P('ctx', 'head')
- key_grad: bfloat16 [4096, 1024], P('ctx', 'head')
- value_grad: bfloat16 [4096, 1024], P('ctx', 'head')
- prefix_keygrads: bfloat16 [128, 1024], P('ctx', 'head')
- prefix_valuegrads: bfloat16 [128, 1024], P('ctx', 'head')
Inputs may be any that keep to these rules, and one draw needn't show every extreme that they name: `response_blocks`: the lengths fill all 128 blocks of the row. Every index of ctx from 1 on begins inside a response that started on the index before it. `prompt_members`: every response, numbered 0 to 15 in order along the row, is listed exactly once.
All inputs are finite; a program needn't handle non-finite values.
Results may differ from a plain program's by a relative error of at most 0.008.
Values may be sent and summed in bfloat16 or wider, within the bound.
A program may use at most 64 MiB of HBM per device.

v0:
```python
import math

import jax
import jax.numpy as jnp
from jax import lax
from jax.sharding import PartitionSpec as P

HD = 128
BLK = 32
PL = 128


def shifted(array, axis, by):
    devices = lax.axis_size(axis)
    pairs = [(i, i + by) for i in range(devices) if 0 <= i + by < devices]
    return lax.ppermute(array, axis, pairs)


def token_tables(response_blocks, prompt_members, first_block, count):
    starts = jnp.cumsum(response_blocks) - response_blocks
    responses = response_blocks.shape[0]
    group = prompt_members.shape[1]
    listed = prompt_members.reshape(-1)
    owner = jnp.arange(listed.shape[0], dtype=jnp.int32) // group
    numbers = jnp.arange(responses, dtype=jnp.int32)
    hits = listed[:, None] == numbers[None, :]
    prompt_of = jnp.sum(jnp.where(hits, owner[:, None], 0), axis=0)
    blocks = first_block + jnp.arange(count, dtype=jnp.int32)
    before = starts[None, :] <= blocks[:, None]
    first = jnp.max(jnp.where(before, starts[None, :], 0), axis=1)
    current = jnp.sum(before.astype(jnp.int32), axis=1) - 1
    chosen = numbers[None, :] == current[:, None]
    prompt_block = jnp.sum(jnp.where(chosen, prompt_of[None, :], 0), axis=1)
    return (jnp.repeat(first * BLK, BLK), jnp.repeat(prompt_block, BLK))


def tile_terms(queries, grads, norms, deltas, keys, values, allowed):
    rows = queries.shape[0]
    cols = keys.shape[0]
    heads = norms.shape[1]
    group = heads // (keys.shape[1] // HD)
    scale = 1.0 / math.sqrt(HD)

    def one_head(head, carry):
        query_acc, key_acc, value_acc = carry
        kv_head = head // group
        query_h = lax.dynamic_slice_in_dim(queries, head * HD, HD, 1)
        grad_h = lax.dynamic_slice_in_dim(grads, head * HD, HD, 1)
        key_h = lax.dynamic_slice_in_dim(keys, kv_head * HD, HD, 1)
        value_h = lax.dynamic_slice_in_dim(values, kv_head * HD, HD, 1)
        norm_h = lax.dynamic_slice_in_dim(norms, head, 1, 1)
        delta_h = lax.dynamic_slice_in_dim(deltas, head, 1, 1)
        logits = jnp.dot(query_h, key_h.T, preferred_element_type=jnp.float32)
        weights = jnp.where(allowed, jnp.exp(logits * scale - norm_h), 0.0)
        weights_b = weights.astype(jnp.bfloat16)
        value_term = jnp.dot(weights_b.T, grad_h, preferred_element_type=jnp.float32)
        dweights = jnp.dot(grad_h, value_h.T, preferred_element_type=jnp.float32)
        dlogits = (weights * (dweights - delta_h)).astype(jnp.bfloat16)
        query_term = jnp.dot(dlogits, key_h, preferred_element_type=jnp.float32)
        key_term = jnp.dot(dlogits.T, query_h, preferred_element_type=jnp.float32)
        query_acc = lax.dynamic_update_slice_in_dim(query_acc, query_term, head * HD, 1)
        old_key = lax.dynamic_slice_in_dim(key_acc, kv_head * HD, HD, 1)
        key_acc = lax.dynamic_update_slice_in_dim(key_acc, old_key + key_term, kv_head * HD, 1)
        old_value = lax.dynamic_slice_in_dim(value_acc, kv_head * HD, HD, 1)
        value_acc = lax.dynamic_update_slice_in_dim(
            value_acc, old_value + value_term, kv_head * HD, 1
        )
        return (query_acc, key_acc, value_acc)

    start = (
        jnp.zeros((rows, queries.shape[1]), jnp.float32),
        jnp.zeros((cols, keys.shape[1]), jnp.float32),
        jnp.zeros((cols, keys.shape[1]), jnp.float32),
    )
    return lax.fori_loop(0, heads, one_head, start)


def add_rows(total, term, offset):
    old = lax.dynamic_slice_in_dim(total, offset, term.shape[0], 0)
    return lax.dynamic_update_slice_in_dim(total, old + term, offset, 0)


def shards(
    query_rows,
    key_rows,
    value_rows,
    attn_output,
    out_grad,
    log_norm,
    prefix_keys,
    prefix_values,
    response_blocks,
    prompt_members,
):
    queries, keys, values, outputs, grads = (
        lax.all_to_all(query_rows, "head", split_axis=1, concat_axis=0, tiled=True),
        lax.all_to_all(key_rows, "head", split_axis=1, concat_axis=0, tiled=True),
        lax.all_to_all(value_rows, "head", split_axis=1, concat_axis=0, tiled=True),
        lax.all_to_all(attn_output, "head", split_axis=1, concat_axis=0, tiled=True),
        lax.all_to_all(out_grad, "head", split_axis=1, concat_axis=0, tiled=True),
    )
    own_heads = queries.shape[1] // HD
    deltas = jnp.einsum(
        "thd,thd->th",
        grads.reshape(-1, own_heads, HD),
        outputs.reshape(-1, own_heads, HD),
        preferred_element_type=jnp.float32,
    )
    tokens = queries.shape[0]
    scale = 1.0 / math.sqrt(HD)
    norms = log_norm.T
    position = lax.axis_index("ctx")
    base = position * tokens
    starts, prompts = token_tables(
        response_blocks, prompt_members, position * (tokens // BLK), tokens // BLK
    )
    local_start = starts - base
    positions = jnp.arange(tokens, dtype=jnp.int32)
    allowed_here = (positions[None, :] >= local_start[:, None]) & (
        positions[None, :] <= positions[:, None]
    )
    allowed_prior = positions[None, :] - tokens >= local_start[:, None]
    query_one, key_one, value_one = tile_terms(
        queries, grads, norms, deltas, keys, values, allowed_here
    )
    keys_prior, values_prior = shifted((keys, values), "ctx", 1)
    query_two, key_two, value_two = tile_terms(
        queries, grads, norms, deltas, keys_prior, values_prior, allowed_prior
    )
    back_keys, back_values = (
        shifted(key_two.astype(jnp.bfloat16), "ctx", -1).astype(key_two.dtype),
        shifted(value_two.astype(jnp.bfloat16), "ctx", -1).astype(value_two.dtype),
    )
    whole_keys, whole_values = (
        lax.all_gather(prefix_keys, "ctx", axis=0, tiled=True),
        lax.all_gather(prefix_values, "ctx", axis=0, tiled=True),
    )
    prompt_total = whole_keys.shape[0]
    prompt_count = prompt_total // PL
    width = prefix_keys.shape[1]
    init = (
        query_one + query_two,
        jnp.zeros((prompt_total, width), jnp.float32),
        jnp.zeros((prompt_total, width), jnp.float32),
    )

    def prompt_step(number, state):
        seen = prompts == number

        def compute(inner):
            total, pkeys, pvalues = inner
            keys_p = lax.dynamic_slice_in_dim(whole_keys, number * PL, PL, 0)
            values_p = lax.dynamic_slice_in_dim(whole_values, number * PL, PL, 0)
            allowed = jnp.broadcast_to(seen[:, None], (tokens, PL))
            query_p, key_p, value_p = tile_terms(
                queries, grads, norms, deltas, keys_p, values_p, allowed
            )
            return (
                total + query_p,
                add_rows(pkeys, key_p, number * PL),
                add_rows(pvalues, value_p, number * PL),
            )

        return lax.cond(jnp.any(seen), compute, lambda inner: inner, state)

    query_total, pkey_acc, pvalue_acc = lax.fori_loop(0, prompt_count, prompt_step, init)
    pkey_sum, pvalue_sum = (
        lax.psum_scatter(pkey_acc, "ctx", scatter_dimension=0, tiled=True),
        lax.psum_scatter(pvalue_acc, "ctx", scatter_dimension=0, tiled=True),
    )
    return (
        (query_total * scale).astype(jnp.bfloat16),
        ((key_one + back_keys) * scale).astype(jnp.bfloat16),
        (value_one + back_values).astype(jnp.bfloat16),
        (pkey_sum * scale).astype(jnp.bfloat16),
        pvalue_sum.astype(jnp.bfloat16),
    )


def solution(mesh):
    placed = (
        P(("ctx", "head"), None),
        P(("ctx", "head"), None),
        P(("ctx", "head"), None),
        P(("ctx", "head"), None),
        P(("ctx", "head"), None),
        P("head", "ctx"),
        P("ctx", "head"),
        P("ctx", "head"),
        P(),
        P(),
    )
    return jax.shard_map(
        shards,
        mesh=mesh,
        in_specs=placed,
        out_specs=(
            P("ctx", "head"),
            P("ctx", "head"),
            P("ctx", "head"),
            P("ctx", "head"),
            P("ctx", "head"),
        ),
        check_vma=False,
    )
```

profile of v0, /device:TPU:0, one launch (start us, length us, event | category | flops | bytes accessed | tf_op | source)
XLA Modules:
  0.0 513.5 jit_solution(17775607721634750118)
XLA Ops:
  8.9 4.2 all-to-all-start.1
  14.9 4.9 all-to-all-done.1
  19.7 4.0 all-to-all-start.3
  25.2 4.6 all-to-all-done.3
  29.9 3.7 all-to-all-start.4
  35.0 15.8 %all-to-all-done.4 = bf16[128,4,1280]{0,2,1:T(8,128)(2,1)S(1)} async-done(((bf16[128,4,1280]{0,2,1:T(8,128)(2,1)}), bf16[128,4,1280]{0,2,1:T(8,128)(2,1)S(1)}, u32[]{:S(2)}, u32[]{:S(2)}) %all-to-all-start.4) | async-done | bytes 1310752 | tf_op jit(solution)/shard_map/all_to_all | solution.py:99
  50.8 3.7 all-to-all-start.2
  54.7 2.5 copy.65
  57.5 14.2 %all-to-all-done.2 = bf16[128,4,1280]{0,2,1:T(8,128)(2,1)S(1)} async-done(((bf16[128,4,1280]{0,2,1:T(8,128)(2,1)}), bf16[128,4,1280]{0,2,1:T(8,128)(2,1)S(1)}, u32[]{:S(2)}, u32[]{:S(2)}) %all-to-all-start.2) | async-done | bytes 1310752 | tf_op jit(solution)/shard_map/all_to_all | solution.py:100
  71.7 4.4 all-to-all-start
  77.9 33.6 %all_gather.6 = bf16[128,256]{1,0:T(8,128)(2,1)} all-gather(bf16[16,256]{1,0:T(8,128)(2,1)S(1)} %copy-done.12), channel_id=1, replica_groups=mesh['ctx'=8,'head'=4] {'ctx'}, dimensions={0}, use_global_device_ids=true | all-gather | bytes 73728 | tf_op jit(solution)/shard_map/all_gather | solution.py:135
  111.6 32.5 %all_gather.7 = bf16[128,256]{1,0:T(8,128)(2,1)} all-gather(bf16[16,256]{1,0:T(8,128)(2,1)S(1)} %copy-done.13), channel_id=1, replica_groups=mesh['ctx'=8,'head'=4] {'ctx'}, dimensions={0}, use_global_device_ids=true | all-gather | bytes 73728 | tf_op jit(solution)/shard_map/all_gather | solution.py:136
  144.1 4.0 collective-permute-start.1
  149.5 7.0 %copy.52 = bf16[4,128,1280]{1,0,2:T(4,128)(2,1)} copy(bf16[4,128,1280]{1,2,0:T(8,128)(2,1)S(1)} %bitcast.73) | data formatting | bytes 2621440 | tf_op jit(solution)/shard_map/all_to_all | solution.py:99
  156.5 3.5 reshape.103
  160.0 6.1 %copy.50 = bf16[4,128,1280]{1,0,2:T(4,128)(2,1)S(1)} copy(bf16[4,128,1280]{1,2,0:T(8,128)(2,1)S(1)} %bitcast.72) | data formatting | bytes 2621440 | tf_op jit(solution)/shard_map/all_to_all | solution.py:100
  168.1 2.1 fusion.67
  172.0 69.1 %while.71 = (s32[]{:T(128)}, f32[512,1280]{1,0:T(8,128)}, f32[512,256]{1,0:T(8,128)S(1)}, f32[512,256]{1,0:T(8,128)S(1)}, bf16[512,1280]{1,0:T(8,128)(2,1)}, /*i...) while((s32[]{:T(128)}, f32[512,1280]{1,0:T(8,128)}, ...), condition=%wide.region_7.8_spmd.clone, body=%wide.region_6.7_spmd.clone.sunk | while | flops 338296832 | bytes 6961539 | solution.py:75
  183.8 2.0 convolution_dynamic-update-slice_fusion.6
  197.6 1.9 convolution_dynamic-update-slice_fusion.6
  204.5 2.0 convolution_dynamic-update-slice_fusion.6
  211.5 2.0 convolution_dynamic-update-slice_fusion.6
  218.4 1.9 convolution_dynamic-update-slice_fusion.6
  225.3 2.0 convolution_dynamic-update-slice_fusion.6
  232.2 2.0 convolution_dynamic-update-slice_fusion.6
  243.6 60.1 %while.72 = (s32[]{:T(128)}, f32[512,1280]{1,0:T(8,128)}, f32[512,256]{1,0:T(8,128)S(1)}, f32[512,256]{1,0:T(8,128)S(1)}, bf16[512,1280]{1,0:T(8,128)(2,1)}, /*i...) while((s32[]{:T(128)}, f32[512,1280]{1,0:T(8,128)}, ...), condition=%wide.region_9.10_spmd.clone, body=%wide.region_8.9_spmd.clone.sunk | while | flops 337772544 | bytes 8012199 | solution.py:75
  305.0 2.8 add.309
  307.9 67.5 %conditional.1 = (f32[512,1280]{1,0:T(8,128)S(1)}, f32[128,256]{1,0:T(8,128)S(1)}, f32[128,256]{1,0:T(8,128)}) conditional(s32[]{:T(128)} %convert_element_type.95, (f32[512,1280]{1,0:T(8,128)S(1)}, f32[128,256]{1,0:T(8,128)S(1)}) %tuple.89, (s32[16]{0:T(128)S(1)}, bf16[512,1280]{1,0:T(8,128)(2,1)}, bf16[128,256]{1,0:T(8,128)(2,1)}, ...), branch_computations={%region_10.11_spmd, %region_11.14_spmd} | conditional | flops 85098528 | bytes 14006971 | solution.py:164
  309.8 62.6 %while.70 = (s32[]{:T(128)}, f32[512,1280]{1,0:T(8,128)}, f32[128,256]{1,0:T(8,128)S(1)}, f32[128,256]{1,0:T(8,128)S(1)}, bf16[512,1280]{1,0:T(8,128)(2,1)}, /*i...) while((s32[]{:T(128)}, f32[512,1280]{1,0:T(8,128)}, ...), condition=%wide.region_13.13_spmd.clone, body=%wide.region_12.12_spmd.clone.sunk | while | flops 84377616 | bytes 2601887 | solution.py:75
  373.1 2.3 add.299
  381.1 57.7 %reduce-scatter.3.cloned.1.call-done = f32[16,256]{1,0:T(8,128)} async-done(((f32[128,256]{1,0:T(8,128)}), f32[16,256]{1,0:T(8,128)}) %reduce-scatter.3.cloned.1.call-update) | async-done | bytes 16400 | tf_op jit(solution)/shard_map/reduce_scatter | solution.py:168
  440.2 62.5 %reduce-scatter.5.cloned.1.call-done = f32[16,256]{1,0:T(8,128)} async-done(((f32[128,256]{1,0:T(8,128)}), f32[16,256]{1,0:T(8,128)}) %reduce-scatter.5.cloned.1.call-update) | async-done | bytes 16400 | tf_op jit(solution)/shard_map/reduce_scatter | solution.py:169
  (296 shorter events, 207.5 us)
Async XLA Ops:
  7.2 16.6 %copy-start.8 = (bf16[128,5120]{1,0:T(8,128)(2,1)S(1)}, bf16[128,5120]{1,0:T(8,128)(2,1)}, u32[]{:S(2)}) copy-start(bf16[128,5120]{1,0:T(8,128)(2,1)} %param.21) | copy-start | bytes 3932164
  8.9 10.8 %all-to-all-start.1 = ((bf16[128,4,256]{2,0,1:T(8,128)(2,1)}), bf16[128,4,256]{2,0,1:T(8,128)(2,1)}, u32[]{:S(2)}, u32[]{:S(2)}) async-start(bf16[128,4,256]{2,0,1:T(8,128)(2,1)} %bitcast.46), calls=%async_computation.1 | async-start | bytes 524288 | tf_op jit(solution)/shard_map/all_to_all | solution.py:97
  19.7 10.1 %all-to-all-start.3 = ((bf16[128,4,256]{2,0,1:T(8,128)(2,1)}), bf16[128,4,256]{2,0,1:T(8,128)(2,1)}, u32[]{:S(2)}, u32[]{:S(2)}) async-start(bf16[128,4,256]{2,0,1:T(8,128)(2,1)} %bitcast.45), calls=%async_computation.3 | async-start | bytes 524288 | tf_op jit(solution)/shard_map/all_to_all | solution.py:98
  29.9 3.7 copy-start.9
  29.9 20.9 %all-to-all-start.4 = ((bf16[128,4,1280]{0,2,1:T(8,128)(2,1)}), bf16[128,4,1280]{0,2,1:T(8,128)(2,1)S(1)}, u32[]{:S(2)}, u32[]{:S(2)}) async-start(bf16[128,4,1280]{0,2,1:T(8,128)(2,1)} %bitcast.13), calls=%async_computation.4 | async-start | bytes 2621440 | tf_op jit(solution)/shard_map/all_to_all | solution.py:99
  50.8 3.7 copy-start.14
  50.8 20.9 %all-to-all-start.2 = ((bf16[128,4,1280]{0,2,1:T(8,128)(2,1)}), bf16[128,4,1280]{0,2,1:T(8,128)(2,1)S(1)}, u32[]{:S(2)}, u32[]{:S(2)}) async-start(bf16[128,4,1280]{0,2,1:T(8,128)(2,1)} %bitcast.75), calls=%async_computation.2 | async-start | bytes 2621440 | tf_op jit(solution)/shard_map/all_to_all | solution.py:100
  54.7 2.7 copy-start.15
  71.7 6.2 %copy-start.12 = (bf16[16,256]{1,0:T(8,128)(2,1)S(1)}, bf16[16,256]{1,0:T(8,128)(2,1)}, u32[]{:S(2)}) copy-start(bf16[16,256]{1,0:T(8,128)(2,1)} %param.24) | copy-start | bytes 24580
  71.7 39.9 %copy-start.13 = (bf16[16,256]{1,0:T(8,128)(2,1)S(1)}, bf16[16,256]{1,0:T(8,128)(2,1)}, u32[]{:S(2)}) copy-start(bf16[16,256]{1,0:T(8,128)(2,1)} %param.25) | copy-start | bytes 24580
  71.7 98.5 %all-to-all-start = ((bf16[128,4,1280]{2,0,1:T(8,128)(2,1)}), bf16[128,4,1280]{2,0,1:T(8,128)(2,1)}, u32[]{:S(2)}, u32[]{:S(2)}) async-start(bf16[128,4,1280]{2,0,1:T(8,128)(2,1)} %bitcast.74), calls=%async_computation | async-start | bytes 2621440 | tf_op jit(solution)/shard_map/all_to_all | solution.py:96
  76.2 362.7 %reduce-scatter.3.cloned.1.call-start = ((), (), s32[]{:S(2)}) async-start(), calls=%async_computation.7 | async-start | bytes 147456 | tf_op jit(solution)/shard_map/reduce_scatter | solution.py:168
  144.1 96.9 %collective-permute-start.1 = (bf16[512,256]{1,0:T(8,128)(2,1)}, bf16[512,256]{1,0:T(8,128)(2,1)}, u32[]{:S(2)}, u32[]{:S(2)}) collective-permute-start(bf16[512,256]{1,0:T(8,128)(2,1)} %bitcast.11), channel_id=1, source_target_pairs={{0,4},{4,8},{8,12},{12,16},{16,20},{20,24},{24,28},{1,5},{5,9},{9,... | collective-permute-start | bytes 786440 | tf_op jit(solution)/shard_map/ppermute | solution.py:16
  148.1 93.0 %collective-permute-start = (bf16[512,256]{1,0:T(8,128)(2,1)}, bf16[512,256]{1,0:T(8,128)(2,1)S(1)}, u32[]{:S(2)}, u32[]{:S(2)}) collective-permute-start(bf16[512,256]{1,0:T(8,128)(2,1)} %bitcast.5), channel_id=1, source_target_pairs={{0,4},{4,8},{8,12},{12,16},{16,20},{20,24},{24,28},{1,5},{5,9},{9,... | collective-permute-start | bytes 786440 | tf_op jit(solution)/shard_map/ppermute | solution.py:16
  241.0 2.5 copy-start.1
  258.8 1.7 copy-start.7
  270.9 1.7 copy-start.7
  276.9 1.7 copy-start.7
  282.9 1.7 copy-start.7
  309.8 5.3 %copy-start.10 = (bf16[128,256]{1,0:T(8,128)(2,1)S(1)}, bf16[128,256]{1,0:T(8,128)(2,1)}, u32[]{:S(2)}) copy-start(bf16[128,256]{1,0:T(8,128)(2,1)} %get-tuple-element.1331) | copy-start | bytes 196612 | tf_op jit(solution)/shard_map/while/body/eval_jaxpr/cond/branch_1_fun/while
  316.0 5.3 %copy-start.10 = (bf16[128,256]{1,0:T(8,128)(2,1)S(1)}, bf16[128,256]{1,0:T(8,128)(2,1)}, u32[]{:S(2)}) copy-start(bf16[128,256]{1,0:T(8,128)(2,1)} %get-tuple-element.1331) | copy-start | bytes 196612 | tf_op jit(solution)/shard_map/while/body/eval_jaxpr/cond/branch_1_fun/while
  322.3 5.3 %copy-start.10 = (bf16[128,256]{1,0:T(8,128)(2,1)S(1)}, bf16[128,256]{1,0:T(8,128)(2,1)}, u32[]{:S(2)}) copy-start(bf16[128,256]{1,0:T(8,128)(2,1)} %get-tuple-element.1331) | copy-start | bytes 196612 | tf_op jit(solution)/shard_map/while/body/eval_jaxpr/cond/branch_1_fun/while
  328.6 5.3 %copy-start.10 = (bf16[128,256]{1,0:T(8,128)(2,1)S(1)}, bf16[128,256]{1,0:T(8,128)(2,1)}, u32[]{:S(2)}) copy-start(bf16[128,256]{1,0:T(8,128)(2,1)} %get-tuple-element.1331) | copy-start | bytes 196612 | tf_op jit(solution)/shard_map/while/body/eval_jaxpr/cond/branch_1_fun/while
  334.8 5.3 %copy-start.10 = (bf16[128,256]{1,0:T(8,128)(2,1)S(1)}, bf16[128,256]{1,0:T(8,128)(2,1)}, u32[]{:S(2)}) copy-start(bf16[128,256]{1,0:T(8,128)(2,1)} %get-tuple-element.1331) | copy-start | bytes 196612 | tf_op jit(solution)/shard_map/while/body/eval_jaxpr/cond/branch_1_fun/while
  341.1 5.3 %copy-start.10 = (bf16[128,256]{1,0:T(8,128)(2,1)S(1)}, bf16[128,256]{1,0:T(8,128)(2,1)}, u32[]{:S(2)}) copy-start(bf16[128,256]{1,0:T(8,128)(2,1)} %get-tuple-element.1331) | copy-start | bytes 196612 | tf_op jit(solution)/shard_map/while/body/eval_jaxpr/cond/branch_1_fun/while
  347.4 5.3 %copy-start.10 = (bf16[128,256]{1,0:T(8,128)(2,1)S(1)}, bf16[128,256]{1,0:T(8,128)(2,1)}, u32[]{:S(2)}) copy-start(bf16[128,256]{1,0:T(8,128)(2,1)} %get-tuple-element.1331) | copy-start | bytes 196612 | tf_op jit(solution)/shard_map/while/body/eval_jaxpr/cond/branch_1_fun/while
  353.6 5.3 %copy-start.10 = (bf16[128,256]{1,0:T(8,128)(2,1)S(1)}, bf16[128,256]{1,0:T(8,128)(2,1)}, u32[]{:S(2)}) copy-start(bf16[128,256]{1,0:T(8,128)(2,1)} %get-tuple-element.1331) | copy-start | bytes 196612 | tf_op jit(solution)/shard_map/while/body/eval_jaxpr/cond/branch_1_fun/while
  359.9 5.3 %copy-start.10 = (bf16[128,256]{1,0:T(8,128)(2,1)S(1)}, bf16[128,256]{1,0:T(8,128)(2,1)}, u32[]{:S(2)}) copy-start(bf16[128,256]{1,0:T(8,128)(2,1)} %get-tuple-element.1331) | copy-start | bytes 196612 | tf_op jit(solution)/shard_map/while/body/eval_jaxpr/cond/branch_1_fun/while
  366.2 5.3 %copy-start.10 = (bf16[128,256]{1,0:T(8,128)(2,1)S(1)}, bf16[128,256]{1,0:T(8,128)(2,1)}, u32[]{:S(2)}) copy-start(bf16[128,256]{1,0:T(8,128)(2,1)} %get-tuple-element.1331) | copy-start | bytes 196612 | tf_op jit(solution)/shard_map/while/body/eval_jaxpr/cond/branch_1_fun/while
  376.1 126.6 %reduce-scatter.5.cloned.1.call-start = ((), (), s32[]{:S(2)}) async-start(), calls=%async_computation.8 | async-start | bytes 147456 | tf_op jit(solution)/shard_map/reduce_scatter | solution.py:169
  377.2 126.8 %collective-permute-start.2 = (bf16[512,256]{1,0:T(8,128)(2,1)S(1)}, bf16[512,256]{1,0:T(8,128)(2,1)}, u32[]{:S(2)}, u32[]{:S(2)}) collective-permute-start(bf16[512,256]{1,0:T(8,128)(2,1)S(1)} %convert_element_type.97), channel_id=1, source_target_pairs={{4,0},{8,4},{12,8},{16,12},{20,16},{24,20},{28,24},{5,1},{9,5},{13... | collective-permute-start | bytes 786440 | tf_op jit(solution)/shard_map/ppermute | solution.py:16
  379.8 126.1 %collective-permute-start.3 = (bf16[512,256]{1,0:T(8,128)(2,1)S(1)}, bf16[512,256]{1,0:T(8,128)(2,1)S(1)}, u32[]{:S(2)}, u32[]{:S(2)}) collective-permute-start(bf16[512,256]{1,0:T(8,128)(2,1)S(1)} %convert_element_type.100), channel_id=1, source_target_pairs={{4,0},{8,4},{12,8},{16,12},{20,16},{24,20},{28,24},{5,1},{9,5},{13... | collective-permute-start | bytes 786440 | tf_op jit(solution)/shard_map/ppermute | solution.py:16
  (13 other events, 17.6 us)
Sparse Core Ops, SparseCore 0:
  376.2 62.6 reduce-scatter.2
  442.8 59.8 reduce-scatter.4
where the time goes:
time: 518 us; the launch traced here: 514 us
  matrix products  168 us (32%)
  waiting for transfers between devices  160 us (31%)
  blocking collectives  66.1 us (13%)
  local copies, waits for them, and re-layouts  58 us (11%)
  starting transfers between devices  28.2 us (5%)
  other arithmetic  16.9 us (3%)
  between operations  14.9 us (3%)
    reduce_scatter x1, waiting for transfers between devices, shards(): lax.psum_scatter(pvalue_acc, 'ctx', scatter_dimension=0, tiled=True)  62.5 us
    reduce_scatter x1, waiting for transfers between devices, shards(): lax.psum_scatter(pkey_acc, 'ctx', scatter_dimension=0, tiled=True)  57.7 us
    dot_general x30, matrix products, one_head(): query_term = jnp.dot(dlogits, key_h, preferred_element_type=jnp.float32)  39.3 us
    dot_general x30, matrix products, one_head(): logits = jnp.dot(query_h, key_h.T, preferred_element_type=jnp.float32)  38.4 us
    dot_general x30, matrix products, one_head(): key_term = jnp.dot(dlogits.T, query_h, preferred_element_type=jnp.float32)  36.7 us
    dot_general x30, matrix products, one_head(): dweights = jnp.dot(grad_h, value_h.T, preferred_element_type=jnp.float32)  35.3 us
    all_gather x1, blocking collectives, shards(): lax.all_gather(prefix_keys, 'ctx', axis=0, tiled=True)  33.6 us
    all_gather x1, blocking collectives, shards(): lax.all_gather(prefix_values, 'ctx', axis=0, tiled=True)  32.5 us
  transfers between devices with their start and end apart: 11, of which 6 were waited for; matrix products, arithmetic and copies ran while one was open for 21% of the time, Pallas kernels for 0%

commit v1 on v0

v1 whole, which is shorter than its diff:
```python
import functools
import math

import jax
import jax.numpy as jnp
from jax import lax
from jax.experimental import pallas as pl
from jax.experimental.pallas import tpu as pltpu
from jax.sharding import PartitionSpec as P

HD = 128
BLK = 32
PL = 128
AHEAD = 3
NEG = -1e30
LOG2E = math.log2(math.e)
F32 = jnp.float32
BF16 = jnp.bfloat16
MESH = pl.DeviceIdType.MESH
NT = (((1,), (1,)), ((), ()))


def kernel(
    q_hbm, k_hbm, v_hbm, o_hbm, g_hbm, norm_ref, pk_ref, pv_ref, blocks_ref, members_ref,
    dq_hbm, dk_ref, dv_ref, dpk_ref, dpv_ref,
    q_all, g_all, k_all, v_all, kp, vp, pk_all, pv_all, kt, g_vm, o_vm,
    dl_send, dl_recv, bias, prompt_of, starts_s,
    dq_acc, dq_out, dk_acc, dv_acc, dkp, dvp, bk_send, bk_recv, pacc, precv,
    q_snd, g_snd, q_rcv, g_rcv, kv_snd, kv_rcv, fw_snd, fw_rcv, pg_snd, pg_rcv,
    pr_snd, pr_rcv, bk_snd_sem, bk_rcv_sem, dl_snd_sem, dl_rcv_sem, loc, dq_sem,
    *, n_ctx, n_head, nprompt, own, kvl,
):
    me = lax.axis_index("head")
    cx = lax.axis_index("ctx")
    rows = q_hbm.shape[0]
    tokens = rows * n_head
    width = own * HD
    kvw = kvl * HD
    grp = own // kvl
    scale = 1.0 / math.sqrt(HD)
    ptot = nprompt * PL
    part = ptot // n_ctx
    nresp = blocks_ref.shape[0]
    members = members_ref.shape[1]
    slot = dl_send.shape[1]
    mine = pl.ds(pl.multiple_of(me * rows, rows), rows)

    def from_rows(s):
        return pl.ds(pl.multiple_of(s * rows, rows), rows)

    def head_cols(dst, h):
        return pl.ds(pl.multiple_of(dst * width + h * HD, HD), HD)

    def kv_cols(dst):
        return pl.ds(pl.multiple_of(dst * kvw, HD), kvw)

    def part_rows(c):
        return pl.ds(pl.multiple_of(c * part, part), part)

    def remote(src, dst, snd, rcv, **to):
        return pltpu.make_async_remote_copy(
            src_ref=src, dst_ref=dst, send_sem=snd, recv_sem=rcv, device_id=to,
            device_id_type=MESH,
        )

    def arrived(ref, sem):
        pltpu.make_async_copy(ref, ref, sem).wait()

    def peer(off):
        return lax.rem(me + off, n_head)

    def q_copy(h, off):
        dst = peer(off)
        return (
            remote(q_hbm.at[:, head_cols(dst, h)], q_all.at[h, mine], q_snd.at[h, dst],
                   q_rcv.at[h, me], head=dst),
            remote(g_hbm.at[:, head_cols(dst, h)], g_all.at[h, mine], g_snd.at[h, dst],
                   g_rcv.at[h, me], head=dst),
        )

    def q_local(h):
        return (
            pltpu.make_async_copy(q_hbm.at[:, head_cols(me, h)], q_all.at[h, mine], q_rcv.at[h, me]),
            pltpu.make_async_copy(g_hbm.at[:, head_cols(me, h)], g_all.at[h, mine], g_rcv.at[h, me]),
        )

    def send_head(h):
        for off in (2, 1, 3):
            for c in q_copy(h, off):
                c.start()
        for c in q_local(h):
            c.start()

    def kv_copy(off):
        dst = peer(off)
        return (
            remote(k_hbm.at[:, kv_cols(dst)], k_all.at[mine], kv_snd.at[0, dst], kv_rcv.at[0, me], head=dst),
            remote(v_hbm.at[:, kv_cols(dst)], v_all.at[mine], kv_snd.at[1, dst], kv_rcv.at[1, me], head=dst),
        )

    def forward(s):
        r = from_rows(s)
        return (
            remote(k_all.at[r], kp.at[r], fw_snd.at[0, s], fw_rcv.at[0, s], ctx=cx + 1),
            remote(v_all.at[r], vp.at[r], fw_snd.at[1, s], fw_rcv.at[1, s], ctx=cx + 1),
        )

    def prefix_copy(off):
        dst = lax.rem(cx + off, n_ctx)
        r = part_rows(cx)
        return (
            remote(pk_ref, pk_all.at[r], pg_snd.at[0, dst], pg_rcv.at[0, cx], ctx=dst),
            remote(pv_ref, pv_all.at[r], pg_snd.at[1, dst], pg_rcv.at[1, cx], ctx=dst),
        )

    def back(kv):
        return remote(bk_send.at[kv], bk_recv.at[kv], bk_snd_sem.at[kv], bk_rcv_sem.at[kv], ctx=cx - 1)

    def reduce_copy(kv, off):
        dst = lax.rem(cx + off, n_ctx)
        return remote(pacc.at[kv, dst], precv.at[kv, cx], pr_snd.at[kv, dst], pr_rcv.at[kv, cx], ctx=dst)

    def delta_copy(off):
        dst = peer(off)
        return remote(dl_send.at[dst], dl_recv.at[me], dl_snd_sem.at[dst], dl_rcv_sem.at[me], head=dst)

    def over_ctx(body):
        def step(off, carry):
            body(off)
            return carry
        lax.fori_loop(1, n_ctx, step, 0)

    barrier = pltpu.get_barrier_semaphore()
    for off in range(1, n_head):
        pl.semaphore_signal(barrier, inc=1, device_id={"head": peer(off)}, device_id_type=MESH)
    over_ctx(lambda off: pl.semaphore_signal(
        barrier, inc=1, device_id={"ctx": lax.rem(cx + off, n_ctx)}, device_id_type=MESH))

    get_g = pltpu.make_async_copy(g_hbm, g_vm, loc.at[0])
    get_o = pltpu.make_async_copy(o_hbm, o_vm, loc.at[1])
    get_g.start()
    get_o.start()
    own_kv = (
        pltpu.make_async_copy(k_hbm.at[:, kv_cols(me)], k_all.at[mine], loc.at[2]),
        pltpu.make_async_copy(v_hbm.at[:, kv_cols(me)], v_all.at[mine], loc.at[3]),
    )
    for c in own_kv:
        c.start()
    pl.semaphore_wait(barrier, n_head - 1 + n_ctx - 1)

    for off in (2, 1, 3):
        for c in kv_copy(off):
            c.start()
    for h in range(AHEAD):
        send_head(h)
    for c in own_kv:
        c.wait()

    @pl.when(cx < n_ctx - 1)
    def _():
        for c in forward(me):
            c.start()

    def prefix_start(off):
        for c in prefix_copy(off):
            c.start()
    over_ctx(prefix_start)
    pk_all[part_rows(cx)] = pk_ref[...]
    pv_all[part_rows(cx)] = pv_ref[...]

    get_g.wait()
    get_o.wait()
    lane = lax.broadcasted_iota(jnp.int32, (rows, HD), 1)
    cols = jnp.zeros((rows, HD), F32)
    for d in range(n_head):
        for j in range(own):
            c = (d * own + j) * HD
            term = g_vm[:, c:c + HD].astype(F32) * o_vm[:, c:c + HD].astype(F32)
            total = jnp.sum(term, axis=1, keepdims=True)
            cols = jnp.where(lane == d * slot + j, total, cols)
    flipped = cols.T
    for d in range(n_head):
        dl_send[d] = flipped[d * slot:(d + 1) * slot]
    dl_recv[me] = dl_send[me]
    for off in (2, 1, 3):
        delta_copy(off).start()

    for off in (1, 3, 2):
        s = peer(off)
        arrived(k_all.at[from_rows(s)], kv_rcv.at[0, s])
        arrived(v_all.at[from_rows(s)], kv_rcv.at[1, s])

        @pl.when(cx < n_ctx - 1)
        def _():
            for c in forward(s):
                c.start()

    def scan(r, total):
        starts_s[r] = total
        return total + blocks_ref[r]
    lax.fori_loop(0, nresp, scan, jnp.int32(0))
    block = cx * (tokens // BLK) + lax.broadcasted_iota(jnp.int32, (1, tokens), 1) // BLK

    def place(i, carry):
        first, owner = carry
        p = i // members
        r = members_ref[p, lax.rem(i, members)]
        low = starts_s[r]
        inside = (block >= low) & (block < low + blocks_ref[r])
        return (jnp.where(inside, low * BLK, first), jnp.where(inside, p, owner))

    zero = jnp.zeros((1, tokens), jnp.int32)
    first, owner = lax.fori_loop(0, nprompt * members, place, (zero, zero))
    prompt_of[...] = owner
    first = first - cx * tokens
    key_at = lax.broadcasted_iota(jnp.int32, (tokens, tokens), 0)
    tok_at = lax.broadcasted_iota(jnp.int32, (tokens, tokens), 1)
    bias[0:tokens] = jnp.where(key_at - tokens >= first, 0.0, NEG)
    bias[tokens:2 * tokens] = jnp.where((key_at >= first) & (key_at <= tok_at), 0.0, NEG)

    def prefix_wait(off):
        s = lax.rem(cx + off, n_ctx)
        arrived(pk_all.at[part_rows(s)], pg_rcv.at[0, s])
        arrived(pv_all.at[part_rows(s)], pg_rcv.at[1, s])
    over_ctx(prefix_wait)
    for off in (1, 3, 2):
        s = peer(off)
        arrived(dl_recv.at[s], dl_rcv_sem.at[s])

    @pl.when(cx > 0)
    def _():
        for s in range(n_head):
            arrived(kp.at[s * rows:(s + 1) * rows], fw_rcv.at[0, s])
            arrived(vp.at[s * rows:(s + 1) * rows], fw_rcv.at[1, s])

    dk_acc[...] = jnp.zeros_like(dk_acc)
    dv_acc[...] = jnp.zeros_like(dv_acc)
    pacc[...] = jnp.zeros_like(pacc)

    @pl.when(cx > 0)
    def _():
        dkp[...] = jnp.zeros_like(dkp)
        dvp[...] = jnp.zeros_like(dvp)

    for kv in range(kvl):
        kc = slice(kv * HD, (kv + 1) * HD)
        kt[:, 0:ptot] = pk_all[:, kc].T
        kt[:, ptot + tokens:ptot + 2 * tokens] = k_all[:, kc].T

        @pl.when(cx > 0)
        def _():
            kt[:, ptot:ptot + tokens] = kp[:, kc].T

        def terms(keys, values, keys_t, qs, gs, norm, delta, mask):
            logits = lax.dot_general(keys, qs, NT, preferred_element_type=F32)
            weights = jnp.exp2(logits * (scale * LOG2E) + (mask - norm))
            weights_b = weights.astype(BF16)
            dv = jnp.dot(weights_b, gs, preferred_element_type=F32)
            dw = lax.dot_general(values, gs, NT, preferred_element_type=F32)
            dl = (weights * (dw - delta)).astype(BF16)
            dk = jnp.dot(dl, qs, preferred_element_type=F32)
            dq = jnp.dot(keys_t, dl, preferred_element_type=F32)
            return dq, dk, dv

        def one_head(i, carry):
            h = kv * grp + i

            @pl.when(h + AHEAD < own)
            def _():
                send_head(h + AHEAD)

            for off in (0, 1, 3, 2):
                s = peer(off)
                arrived(q_all.at[h, from_rows(s)], q_rcv.at[h, s])
                arrived(g_all.at[h, from_rows(s)], g_rcv.at[h, s])
            norm = norm_ref[pl.ds(h, 1), :] * LOG2E
            delta = jnp.concatenate(
                [dl_recv[s, pl.ds(h, 1), :] for s in range(n_head)], axis=1)
            qs = q_all[h]
            gs = g_all[h]

            def prompt(p, carry):
                r = pl.ds(pl.multiple_of(p * PL, PL), PL)
                if nprompt == 1:
                    mask = 0.0
                else:
                    mask = jnp.where(prompt_of[...] == p, 0.0, NEG)
                dq, dk, dv = terms(pk_all[r, kc], pv_all[r, kc], kt[:, r], qs, gs, norm, delta, mask)
                c = pl.ds(p * (PL // part), PL // part)
                pacc[kv, c, 0] += dk.reshape(PL // part, part, HD)
                pacc[kv, c, 1] += dv.reshape(PL // part, part, HD)
                if nprompt == 1:
                    dq_acc[...] = dq
                else:
                    dq_acc[...] += dq
                return carry

            if nprompt == 1:
                prompt(0, 0)
            else:
                dq_acc[...] = jnp.zeros_like(dq_acc)
                lax.fori_loop(0, nprompt, prompt, 0)

            kb = tokens // 2
            for b in range(2):
                a, e = b * kb, (b + 1) * kb
                t = slice(a, tokens)
                dq, dk, dv = terms(
                    k_all[a:e, kc], v_all[a:e, kc], kt[:, ptot + tokens + a:ptot + tokens + e],
                    qs[t], gs[t], norm[:, t], delta[:, t], bias[tokens + a:tokens + e, t])
                dk_acc[kv, a:e] += dk
                dv_acc[kv, a:e] += dv
                dq_acc[:, t] += dq

            @pl.when(cx > 0)
            def _():
                for b in range(2):
                    a, e = b * kb, (b + 1) * kb
                    dq, dk, dv = terms(
                        kp[a:e, kc], vp[a:e, kc], kt[:, ptot + a:ptot + e],
                        qs, gs, norm, delta, bias[a:e])
                    dkp[kv, a:e] += dk
                    dvp[kv, a:e] += dv
                    dq_acc[...] += dq

            dq_out[h] = (dq_acc[...] * scale).T.astype(BF16)
            pltpu.make_async_copy(
                dq_out.at[h], dq_hbm.at[:, pl.ds(pl.multiple_of(h * HD, HD), HD)], dq_sem.at[h]
            ).start()
            return carry

        lax.fori_loop(0, grp, one_head, 0)

        @pl.when(cx > 0)
        def _():
            bk_send[kv, 0] = dkp[kv].astype(BF16)
            bk_send[kv, 1] = dvp[kv].astype(BF16)
            back(kv).start()

        over_ctx(lambda off: reduce_copy(kv, off).start())
        precv[kv, cx] = pacc[kv, cx]

    for kv in range(kvl):
        kc = slice(kv * HD, (kv + 1) * HD)

        def sum_wait(off):
            s = lax.rem(cx + off, n_ctx)
            arrived(precv.at[kv, s], pr_rcv.at[kv, s])
        over_ctx(sum_wait)
        total = lax.fori_loop(0, n_ctx, lambda s, t: t + precv[kv, s], jnp.zeros((2, part, HD), F32))
        dpk_ref[:, kc] = (total[0] * scale).astype(BF16)
        dpv_ref[:, kc] = total[1].astype(BF16)

        @pl.when(cx < n_ctx - 1)
        def _():
            arrived(bk_recv.at[kv], bk_rcv_sem.at[kv])
            dk_ref[:, kc] = ((dk_acc[kv] + bk_recv[kv, 0].astype(F32)) * scale).astype(BF16)
            dv_ref[:, kc] = (dv_acc[kv] + bk_recv[kv, 1].astype(F32)).astype(BF16)

        @pl.when(cx == n_ctx - 1)
        def _():
            dk_ref[:, kc] = (dk_acc[kv] * scale).astype(BF16)
            dv_ref[:, kc] = dv_acc[kv].astype(BF16)

    def finish(h, carry):
        pltpu.make_async_copy(
            dq_out.at[h], dq_hbm.at[:, pl.ds(pl.multiple_of(h * HD, HD), HD)], dq_sem.at[h]
        ).wait()
        for off in (2, 1, 3):
            for c in q_copy(h, off):
                c.wait_send()
        return carry
    lax.fori_loop(0, own, finish, 0)
    for off in (2, 1, 3):
        for c in kv_copy(off):
            c.wait_send()
        delta_copy(off).wait_send()

    @pl.when(cx < n_ctx - 1)
    def _():
        for s in range(n_head):
            for c in forward(s):
                c.wait_send()

    @pl.when(cx > 0)
    def _():
        for kv in range(kvl):
            back(kv).wait_send()

    def sent(off):
        for c in prefix_copy(off):
            c.wait_send()
        for kv in range(kvl):
            reduce_copy(kv, off).wait_send()
    over_ctx(sent)


def shards(n_ctx, n_head, *arrays):
    query_rows, key_rows, _, _, _, log_norm, prefix_keys, _, blocks, members = arrays
    rows, total_width = query_rows.shape
    own = log_norm.shape[0]
    kvw = prefix_keys.shape[1]
    kvl = kvw // HD
    tokens = rows * n_head
    nprompt = members.shape[0]
    ptot = nprompt * PL
    part = prefix_keys.shape[0]
    slot = -(-own // 8) * 8
    hbm = pl.BlockSpec(memory_space=pl.ANY)
    vmem = pl.BlockSpec(memory_space=pltpu.VMEM)
    smem = pl.BlockSpec(memory_space=pltpu.SMEM)
    dma = pltpu.SemaphoreType.DMA
    return pl.pallas_call(
        functools.partial(
            kernel, n_ctx=n_ctx, n_head=n_head, nprompt=nprompt, own=own, kvl=kvl),
        out_shape=(
            jax.ShapeDtypeStruct((tokens, own * HD), BF16),
            jax.ShapeDtypeStruct((tokens, kvw), BF16),
            jax.ShapeDtypeStruct((tokens, kvw), BF16),
            jax.ShapeDtypeStruct((part, kvw), BF16),
            jax.ShapeDtypeStruct((part, kvw), BF16),
        ),
        in_specs=[hbm] * 5 + [vmem] * 3 + [smem] * 2,
        out_specs=(hbm, vmem, vmem, vmem, vmem),
        scratch_shapes=[
            pltpu.VMEM((own, tokens, HD), BF16),
            pltpu.VMEM((own, tokens, HD), BF16),
            pltpu.VMEM((tokens, kvw), BF16),
            pltpu.VMEM((tokens, kvw), BF16),
            pltpu.VMEM((tokens, kvw), BF16),
            pltpu.VMEM((tokens, kvw), BF16),
            pltpu.VMEM((ptot, kvw), BF16),
            pltpu.VMEM((ptot, kvw), BF16),
            pltpu.VMEM((HD, ptot + 2 * tokens), BF16),
            pltpu.VMEM((rows, total_width), BF16),
            pltpu.VMEM((rows, total_width), BF16),
            pltpu.VMEM((n_head, slot, rows), F32),
            pltpu.VMEM((n_head, slot, rows), F32),
            pltpu.VMEM((2 * tokens, tokens), F32),
            pltpu.VMEM((1, tokens), jnp.int32),
            pltpu.SMEM(blocks.shape, jnp.int32),
            pltpu.VMEM((HD, tokens), F32),
            pltpu.VMEM((own, tokens, HD), BF16),
            pltpu.VMEM((kvl, tokens, HD), F32),
            pltpu.VMEM((kvl, tokens, HD), F32),
            pltpu.VMEM((kvl, tokens, HD), F32),
            pltpu.VMEM((kvl, tokens, HD), F32),
            pltpu.VMEM((kvl, 2, tokens, HD), BF16),
            pltpu.VMEM((kvl, 2, tokens, HD), BF16),
            pltpu.VMEM((kvl, n_ctx, 2, part, HD), F32),
            pltpu.VMEM((kvl, n_ctx, 2, part, HD), F32),
            dma((own, n_head)), dma((own, n_head)), dma((own, n_head)), dma((own, n_head)),
            dma((2, n_head)), dma((2, n_head)), dma((2, n_head)), dma((2, n_head)),
            dma((2, n_ctx)), dma((2, n_ctx)),
            dma((kvl, n_ctx)), dma((kvl, n_ctx)),
            dma((kvl,)), dma((kvl,)),
            dma((n_head,)), dma((n_head,)),
            dma((4,)), dma((own,)),
        ],
        compiler_params=pltpu.CompilerParams(
            collective_id=0, has_side_effects=True, vmem_limit_bytes=48 * 1024 * 1024),
    )(*arrays)


def solution(mesh):
    placed = (
        P(("ctx", "head"), None),
        P(("ctx", "head"), None),
        P(("ctx", "head"), None),
        P(("ctx", "head"), None),
        P(("ctx", "head"), None),
        P("head", "ctx"),
        P("ctx", "head"),
        P("ctx", "head"),
        P(),
        P(),
    )
    return jax.shard_map(
        functools.partial(shards, mesh.shape["ctx"], mesh.shape["head"]),
        mesh=mesh,
        in_specs=placed,
        out_specs=(
            P("ctx", "head"),
            P("ctx", "head"),
            P("ctx", "head"),
            P("ctx", "head"),
            P("ctx", "head"),
        ),
        check_vma=False,
    )
```

time: 518 us -> 74.4 us (0.14)
  matrix products: 168 us -> 0 us
  waiting for transfers between devices: 160 us -> 0 us
  blocking collectives: 66.1 us -> 0 us
  Pallas kernels: 0 us -> 61.7 us
  local copies, waits for them, and re-layouts: 58 us -> 11.6 us
  starting transfers between devices: 28.2 us -> 0 us
  other arithmetic: 16.9 us -> 0 us
  between operations: 14.9 us -> 0.66 us
    dot_general x150 -> x0, matrix products: 168 us -> none  [the longest x30 39.3 us: one_head(): query_term = jnp.dot(dlogits, key_h, preferred_element_type=jnp.float32)]
    reduce_scatter x2 -> x0, waiting for transfers between devices: 120 us -> none  [the longest x1 62.5 us: shards(): lax.psum_scatter(pvalue_acc, 'ctx', scatter_dimension=0, tiled=True)]
    all_gather x2 -> x0, blocking collectives: 66.1 us -> none  [the longest x1 33.6 us: shards(): lax.all_gather(prefix_keys, 'ctx', axis=0, tiled=True)]
    pallas_call x0 -> x1, Pallas kernels: none -> 61.7 us  [shards(): pl.pallas_call(functools.partial(kernel, n_ctx=n_ctx, n_head=n_head, npro...]
    all_to_all x5 -> x0, waiting for transfers between devices: 39.5 us -> none  [the longest x1 15.8 us: shards(): lax.all_to_all(attn_output, 'head', split_axis=1, concat_axis=0, tiled=True)]
    dynamic_slice x30 -> x0, local copies, waits for them, and re-layouts: 22.2 us -> none  [one_head(): delta_h = lax.dynamic_slice_in_dim(deltas, head, 1, 1)]
    all_to_all x5 -> x0, starting transfers between devices: 20.1 us -> none  [the longest x1 4.45 us: shards(): lax.all_to_all(query_rows, 'head', split_axis=1, concat_axis=0, tiled=True)]
    all_to_all x6 -> x0, local copies, waits for them, and re-layouts: 19.6 us -> none  [the longest x1 6.97 us: shards(): lax.all_to_all(attn_output, 'head', split_axis=1, concat_axis=0, tiled=True)]
  transfers between devices with their start and end apart: 11 -> 0, of which waited for: 6 -> 0; matrix products, arithmetic and copies ran while one was open for 21% -> 0% of each run, Pallas kernels for 0% -> 0%
where the time goes in v1:
time: 74.4 us; the launch traced here: 74 us
  Pallas kernels  61.7 us (83%)
  local copies, waits for them, and re-layouts  11.6 us (16%)
    pallas_call x1, Pallas kernels, shards(): pl.pallas_call(functools.partial(kernel, n_ctx=n_ctx, n_head=n_head, npro...  61.7 us
    unnamed x23, local copies, waits for them, and re-layouts  11.6 us

profile of v1, /device:TPU:0, one launch (start us, length us, event | category | flops | bytes accessed | tf_op | source)
XLA Modules:
  0.0 74.0 jit_solution(13163520589870124067)
XLA Ops:
  0.6 0.0 copy-start
  0.6 1.3 %copy-done = bf16[128,5120]{1,0:T(8,128)(2,1)S(1)} copy-done((bf16[128,5120]{1,0:T(8,128)(2,1)S(1)}, bf16[128,5120]{1,0:T(8,128)(2,1)}, u32[]{:S(2)}) %copy-start) | copy-done | bytes 1310744
  2.0 0.0 copy-start.1
  2.0 1.3 %copy-done.1 = bf16[128,5120]{1,0:T(8,128)(2,1)S(1)} copy-done((bf16[128,5120]{1,0:T(8,128)(2,1)S(1)}, bf16[128,5120]{1,0:T(8,128)(2,1)}, u32[]{:S(2)}) %copy-start.1) | copy-done | bytes 1310744
  3.3 0.0 copy-start.2
  3.3 0.9 %copy-done.2 = bf16[128,1024]{1,0:T(8,128)(2,1)S(1)} copy-done((bf16[128,1024]{1,0:T(8,128)(2,1)S(1)}, bf16[128,1024]{1,0:T(8,128)(2,1)}, u32[]{:S(2)}) %copy-start.2) | copy-done | bytes 262168
  4.2 0.0 copy-start.3
  4.2 0.9 %copy-done.3 = bf16[128,1024]{1,0:T(8,128)(2,1)S(1)} copy-done((bf16[128,1024]{1,0:T(8,128)(2,1)S(1)}, bf16[128,1024]{1,0:T(8,128)(2,1)}, u32[]{:S(2)}) %copy-start.3) | copy-done | bytes 262168
  5.2 0.0 copy-start.4
  5.2 0.8 %copy-done.4 = f32[10,512]{1,0:T(8,128)S(1)} copy-done((f32[10,512]{1,0:T(8,128)S(1)}, f32[10,512]{1,0:T(8,128)}, u32[]{:S(2)}) %copy-start.4) | copy-done | bytes 20504
  5.9 0.0 copy-start.5
  5.9 0.7 copy-done.5
  6.6 0.0 copy-start.6
  6.6 0.7 copy-done.6
  7.3 0.0 copy-start.7
  7.3 0.7 copy-done.7
  8.0 0.0 copy-start.8
  8.0 0.7 copy-done.8
  8.6 61.7 %shard_map.137 = (bf16[512,1280]{1,0:T(8,128)(2,1)S(1)}, bf16[512,256]{1,0:T(8,128)(2,1)S(1)}, bf16[512,256]{1,0:T(8,128)(2,1)S(1)}, bf16[16,256]{1,0:T(8,128)(2,1)S(1)}, bf16[16,256]{1,0:T(8,128)(2,1)S(1)}) custom-call(bf16[128,5120]{1,0:T(8,128)(2,1)S(1)} %copy-done, bf16[128,1024]{1,0:T(8,128)(2,1)S(1)} %copy-done.2, bf16[128,1024]{1,0:T(8,128)(2,1)S(1)} %copy-done.3, ...), custom_call_target="tpu_custom_call" | custom-call | tf_op jit(solution)/shard_map/pallas_call | solution.py:413
  70.3 1.1 %copy.20 = bf16[512,1280]{1,0:T(8,128)(2,1)} copy(bf16[512,1280]{1,0:T(8,128)(2,1)S(1)} %get-tuple-element.10) | data formatting | bytes 2621440
  71.4 0.7 copy.21
  72.1 0.7 copy.22
  72.8 0.6 copy.23
  73.4 0.6 copy.24
Async XLA Ops:
  0.6 1.3 %copy-start = (bf16[128,5120]{1,0:T(8,128)(2,1)S(1)}, bf16[128,5120]{1,0:T(8,128)(2,1)}, u32[]{:S(2)}) copy-start(bf16[128,5120]{1,0:T(8,128)(2,1)} %q_hbm.1) | copy-start | bytes 3932164
  2.0 1.3 %copy-start.1 = (bf16[128,5120]{1,0:T(8,128)(2,1)S(1)}, bf16[128,5120]{1,0:T(8,128)(2,1)}, u32[]{:S(2)}) copy-start(bf16[128,5120]{1,0:T(8,128)(2,1)} %o_hbm.1) | copy-start | bytes 3932164
  3.3 0.9 %copy-start.2 = (bf16[128,1024]{1,0:T(8,128)(2,1)S(1)}, bf16[128,1024]{1,0:T(8,128)(2,1)}, u32[]{:S(2)}) copy-start(bf16[128,1024]{1,0:T(8,128)(2,1)} %k_hbm.1) | copy-start | bytes 786436
  4.2 0.9 %copy-start.3 = (bf16[128,1024]{1,0:T(8,128)(2,1)S(1)}, bf16[128,1024]{1,0:T(8,128)(2,1)}, u32[]{:S(2)}) copy-start(bf16[128,1024]{1,0:T(8,128)(2,1)} %v_hbm.1) | copy-start | bytes 786436
  5.2 0.8 %copy-start.4 = (f32[10,512]{1,0:T(8,128)S(1)}, f32[10,512]{1,0:T(8,128)}, u32[]{:S(2)}) copy-start(f32[10,512]{1,0:T(8,128)} %norm_ref.1) | copy-start | bytes 61444
  5.9 0.7 copy-start.5
  6.6 0.7 copy-start.6
  7.3 0.7 copy-start.7
  8.0 0.7 copy-start.8

commit v2 on v1

--- a/solution.py
+++ b/solution.py
@@ -11,7 +11,11 @@
 HD = 128
 BLK = 32
 PL = 128
+EARLY = 1
 AHEAD = 3
+LAG = 2
+PIECES = 4
+VMEM_BYTES = 60 * 1024 * 1024
 NEG = -1e30
 LOG2E = math.log2(math.e)
 F32 = jnp.float32
@@ -21,11 +25,11 @@
 
 
 def kernel(
-    q_hbm, k_hbm, v_hbm, o_hbm, g_hbm, norm_ref, pk_ref, pv_ref, blocks_ref, members_ref,
+    q_hbm, k_hbm, v_hbm, o_hbm, g_hbm, norm_hbm, pk_ref, pv_ref, blocks_hbm, members_hbm,
     dq_hbm, dk_ref, dv_ref, dpk_ref, dpv_ref,
     q_all, g_all, k_all, v_all, kp, vp, pk_all, pv_all, kt, g_vm, o_vm,
-    dl_send, dl_recv, bias, prompt_of, starts_s,
-    dq_acc, dq_out, dk_acc, dv_acc, dkp, dvp, bk_send, bk_recv, pacc, precv,
+    norm_ref, blocks_ref, members_ref, dl_send, dl_recv, bias, prompt_of, starts_s,
+    dq_acc, dq_out, dk_acc, dv_acc, dkp, dvp, bk_send, bk_recv, pacc, psend, precv,
     q_snd, g_snd, q_rcv, g_rcv, kv_snd, kv_rcv, fw_snd, fw_rcv, pg_snd, pg_rcv,
     pr_snd, pr_rcv, bk_snd_sem, bk_rcv_sem, dl_snd_sem, dl_rcv_sem, loc, dq_sem,
     *, n_ctx, n_head, nprompt, own, kvl,
@@ -118,7 +122,7 @@
 
     def reduce_copy(kv, off):
         dst = lax.rem(cx + off, n_ctx)
-        return remote(pacc.at[kv, dst], precv.at[kv, cx], pr_snd.at[kv, dst], pr_rcv.at[kv, cx], ctx=dst)
+        return remote(psend.at[kv, dst], precv.at[kv, cx], pr_snd.at[kv, dst], pr_rcv.at[kv, cx], ctx=dst)
 
     def delta_copy(off):
         dst = peer(off)
@@ -140,6 +144,15 @@
     get_o = pltpu.make_async_copy(o_hbm, o_vm, loc.at[1])
     get_g.start()
     get_o.start()
+    small = (
+        pltpu.make_async_copy(norm_hbm, norm_ref, loc.at[4]),
+        pltpu.make_async_copy(blocks_hbm, blocks_ref, loc.at[5]),
+        pltpu.make_async_copy(members_hbm, members_ref, loc.at[6]),
+        pltpu.make_async_copy(pk_ref, pk_all.at[part_rows(cx)], loc.at[7]),
+        pltpu.make_async_copy(pv_ref, pv_all.at[part_rows(cx)], loc.at[8]),
+    )
+    for c in small:
+        c.start()
     own_kv = (
         pltpu.make_async_copy(k_hbm.at[:, kv_cols(me)], k_all.at[mine], loc.at[2]),
         pltpu.make_async_copy(v_hbm.at[:, kv_cols(me)], v_all.at[mine], loc.at[3]),
@@ -151,8 +164,6 @@
     for off in (2, 1, 3):
         for c in kv_copy(off):
             c.start()
-    for h in range(AHEAD):
-        send_head(h)
     for c in own_kv:
         c.wait()
 
@@ -165,8 +176,8 @@
         for c in prefix_copy(off):
             c.start()
     over_ctx(prefix_start)
-    pk_all[part_rows(cx)] = pk_ref[...]
-    pv_all[part_rows(cx)] = pv_ref[...]
+    for h in range(EARLY):
+        send_head(h)
 
     get_g.wait()
     get_o.wait()
@@ -195,6 +206,11 @@
             for c in forward(s):
                 c.start()
 
+    for h in range(EARLY, AHEAD):
+        send_head(h)
+    for c in small:
+        c.wait()
+
     def scan(r, total):
         starts_s[r] = total
         return total + blocks_ref[r]
@@ -222,16 +238,9 @@
         s = lax.rem(cx + off, n_ctx)
         arrived(pk_all.at[part_rows(s)], pg_rcv.at[0, s])
         arrived(pv_all.at[part_rows(s)], pg_rcv.at[1, s])
-    over_ctx(prefix_wait)
     for off in (1, 3, 2):
         s = peer(off)
         arrived(dl_recv.at[s], dl_rcv_sem.at[s])
-
-    @pl.when(cx > 0)
-    def _():
-        for s in range(n_head):
-            arrived(kp.at[s * rows:(s + 1) * rows], fw_rcv.at[0, s])
-            arrived(vp.at[s * rows:(s + 1) * rows], fw_rcv.at[1, s])
 
     dk_acc[...] = jnp.zeros_like(dk_acc)
     dv_acc[...] = jnp.zeros_like(dv_acc)
@@ -242,103 +251,154 @@
         dkp[...] = jnp.zeros_like(dkp)
         dvp[...] = jnp.zeros_like(dvp)
 
-    for kv in range(kvl):
+    def terms(keys, values, keys_t, qs, gs, norm, delta, mask):
+        logits = lax.dot_general(keys, qs, NT, preferred_element_type=F32)
+        weights = jnp.exp2(logits * (scale * LOG2E) + (mask - norm))
+        weights_b = weights.astype(BF16)
+        dv = jnp.dot(weights_b, gs, preferred_element_type=F32)
+        dw = lax.dot_general(values, gs, NT, preferred_element_type=F32)
+        dl = (weights * (dw - delta)).astype(BF16)
+        dk = jnp.dot(dl, qs, preferred_element_type=F32)
+        dq = jnp.dot(keys_t, dl, preferred_element_type=F32)
+        return dq, dk, dv
+
+    def of_head(h):
+        norm = norm_ref[pl.ds(h, 1), :] * LOG2E
+        delta = jnp.concatenate([dl_recv[s, pl.ds(h, 1), :] for s in range(n_head)], axis=1)
+        return q_all[h], g_all[h], norm, delta
+
+    kb = tokens // 2
+
+    def add_dq(h, t, dq, first):
+        if first:
+            dq_acc[h, :, t] = dq
+        else:
+            dq_acc[h, :, t] += dq
+
+    def here(kv, h, first):
         kc = slice(kv * HD, (kv + 1) * HD)
-        kt[:, 0:ptot] = pk_all[:, kc].T
-        kt[:, ptot + tokens:ptot + 2 * tokens] = k_all[:, kc].T
+        qs, gs, norm, delta = of_head(h)
+        for b in range(2):
+            a, e = b * kb, (b + 1) * kb
+            t = slice(a, tokens)
+            dq, dk, dv = terms(
+                k_all[a:e, kc], v_all[a:e, kc], kt[:, ptot + tokens + a:ptot + tokens + e],
+                qs[t], gs[t], norm[:, t], delta[:, t], bias[tokens + a:tokens + e, t])
+            dk_acc[kv, a:e] += dk
+            dv_acc[kv, a:e] += dv
+            add_dq(h, t, dq, first and b == 0)
+
+    def elsewhere(kv, h, first):
+        kc = slice(kv * HD, (kv + 1) * HD)
+        every = slice(0, tokens)
+
+        def prompt(p, sets):
+            qs, gs, norm, delta = of_head(h)
+            r = pl.ds(pl.multiple_of(p * PL, PL), PL)
+            if nprompt == 1:
+                mask = 0.0
+            else:
+                mask = jnp.where(prompt_of[...] == p, 0.0, NEG)
+            dq, dk, dv = terms(pk_all[r, kc], pv_all[r, kc], kt[:, r], qs, gs, norm, delta, mask)
+            c = pl.ds(p * (PL // part), PL // part)
+            pacc[kv, c, 0] += dk.reshape(PL // part, part, HD)
+            pacc[kv, c, 1] += dv.reshape(PL // part, part, HD)
+            add_dq(h, every, dq, sets)
+
+        prompt(0, first)
+        if nprompt > 1:
+            def more(p, carry):
+                prompt(p, False)
+                return carry
+            lax.fori_loop(1, nprompt, more, 0)
 
         @pl.when(cx > 0)
         def _():
-            kt[:, ptot:ptot + tokens] = kp[:, kc].T
-
-        def terms(keys, values, keys_t, qs, gs, norm, delta, mask):
-            logits = lax.dot_general(keys, qs, NT, preferred_element_type=F32)
-            weights = jnp.exp2(logits * (scale * LOG2E) + (mask - norm))
-            weights_b = weights.astype(BF16)
-            dv = jnp.dot(weights_b, gs, preferred_element_type=F32)
-            dw = lax.dot_general(values, gs, NT, preferred_element_type=F32)
-            dl = (weights * (dw - delta)).astype(BF16)
-            dk = jnp.dot(dl, qs, preferred_element_type=F32)
-            dq = jnp.dot(keys_t, dl, preferred_element_type=F32)
-            return dq, dk, dv
-
-        def one_head(i, carry):
-            h = kv * grp + i
-
-            @pl.when(h + AHEAD < own)
-            def _():
-                send_head(h + AHEAD)
-
-            for off in (0, 1, 3, 2):
-                s = peer(off)
-                arrived(q_all.at[h, from_rows(s)], q_rcv.at[h, s])
-                arrived(g_all.at[h, from_rows(s)], g_rcv.at[h, s])
-            norm = norm_ref[pl.ds(h, 1), :] * LOG2E
-            delta = jnp.concatenate(
-                [dl_recv[s, pl.ds(h, 1), :] for s in range(n_head)], axis=1)
-            qs = q_all[h]
-            gs = g_all[h]
-
-            def prompt(p, carry):
-                r = pl.ds(pl.multiple_of(p * PL, PL), PL)
-                if nprompt == 1:
-                    mask = 0.0
-                else:
-                    mask = jnp.where(prompt_of[...] == p, 0.0, NEG)
-                dq, dk, dv = terms(pk_all[r, kc], pv_all[r, kc], kt[:, r], qs, gs, norm, delta, mask)
-                c = pl.ds(p * (PL // part), PL // part)
-                pacc[kv, c, 0] += dk.reshape(PL // part, part, HD)
-                pacc[kv, c, 1] += dv.reshape(PL // part, part, HD)
-                if nprompt == 1:
-                    dq_acc[...] = dq
-                else:
-                    dq_acc[...] += dq
-                return carry
-
-            if nprompt == 1:
-                prompt(0, 0)
-            else:
-                dq_acc[...] = jnp.zeros_like(dq_acc)
-                lax.fori_loop(0, nprompt, prompt, 0)
-
-            kb = tokens // 2
+            qs, gs, norm, delta = of_head(h)
             for b in range(2):
                 a, e = b * kb, (b + 1) * kb
-                t = slice(a, tokens)
                 dq, dk, dv = terms(
-                    k_all[a:e, kc], v_all[a:e, kc], kt[:, ptot + tokens + a:ptot + tokens + e],
-                    qs[t], gs[t], norm[:, t], delta[:, t], bias[tokens + a:tokens + e, t])
-                dk_acc[kv, a:e] += dk
-                dv_acc[kv, a:e] += dv
-                dq_acc[:, t] += dq
-
-            @pl.when(cx > 0)
-            def _():
-                for b in range(2):
-                    a, e = b * kb, (b + 1) * kb
-                    dq, dk, dv = terms(
-                        kp[a:e, kc], vp[a:e, kc], kt[:, ptot + a:ptot + e],
-                        qs, gs, norm, delta, bias[a:e])
-                    dkp[kv, a:e] += dk
-                    dvp[kv, a:e] += dv
-                    dq_acc[...] += dq
-
-            dq_out[h] = (dq_acc[...] * scale).T.astype(BF16)
-            pltpu.make_async_copy(
-                dq_out.at[h], dq_hbm.at[:, pl.ds(pl.multiple_of(h * HD, HD), HD)], dq_sem.at[h]
-            ).start()
-            return carry
-
-        lax.fori_loop(0, grp, one_head, 0)
-
+                    kp[a:e, kc], vp[a:e, kc], kt[:, ptot + a:ptot + e],
+                    qs, gs, norm, delta, bias[a:e])
+                dkp[kv, a:e] += dk
+                dvp[kv, a:e] += dv
+                add_dq(h, every, dq, False)
+
+    def give_back(kv):
         @pl.when(cx > 0)
         def _():
             bk_send[kv, 0] = dkp[kv].astype(BF16)
             bk_send[kv, 1] = dvp[kv].astype(BF16)
             back(kv).start()
-
+        psend[kv] = pacc[kv].astype(BF16)
         over_ctx(lambda off: reduce_copy(kv, off).start())
-        precv[kv, cx] = pacc[kv, cx]
+
+    def write_dq(h):
+        dq_out[h] = (dq_acc[h] * scale).T.astype(BF16)
+        pltpu.make_async_copy(
+            dq_out.at[h], dq_hbm.at[:, pl.ds(pl.multiple_of(h * HD, HD), HD)], dq_sem.at[h]
+        ).start()
+
+    def take_head(h):
+        @pl.when(h + AHEAD < own)
+        def _():
+            send_head(h + AHEAD)
+        for off in (0, 1, 3, 2):
+            s = peer(off)
+            arrived(q_all.at[h, from_rows(s)], q_rcv.at[h, s])
+            arrived(g_all.at[h, from_rows(s)], g_rcv.at[h, s])
+
+    def keys_from_elsewhere(kv):
+        kc = slice(kv * HD, (kv + 1) * HD)
+        if kv == 0:
+            over_ctx(prefix_wait)
+        kt[:, 0:ptot] = pk_all[:, kc].T
+
+        @pl.when(cx > 0)
+        def _():
+            if kv == 0:
+                for s in range(n_head):
+                    arrived(kp.at[s * rows:(s + 1) * rows], fw_rcv.at[0, s])
+                    arrived(vp.at[s * rows:(s + 1) * rows], fw_rcv.at[1, s])
+            kt[:, ptot:ptot + tokens] = kp[:, kc].T
+
+    for kv in range(kvl):
+        kt[:, ptot + tokens:ptot + 2 * tokens] = k_all[:, kv * HD:(kv + 1) * HD].T
+        if kv > 0:
+            keys_from_elsewhere(kv)
+
+        def step(i, carry):
+            h = kv * grp + i
+
+            @pl.when(i < grp)
+            def _():
+                take_head(h)
+                if kv == 0:
+                    here(kv, h, True)
+                else:
+                    elsewhere(kv, h, True)
+
+            if kv == 0:
+                @pl.when(i == LAG)
+                def _():
+                    keys_from_elsewhere(kv)
+            else:
+                @pl.when(i == grp - 1)
+                def _():
+                    give_back(kv)
+
+            @pl.when(i >= LAG)
+            def _():
+                if kv == 0:
+                    elsewhere(kv, h - LAG, False)
+                else:
+                    here(kv, h - LAG, False)
+                write_dq(h - LAG)
+            return carry
+
+        lax.fori_loop(0, grp + LAG, step, 0)
+        if kv == 0:
+            give_back(kv)
 
     for kv in range(kvl):
         kc = slice(kv * HD, (kv + 1) * HD)
@@ -347,7 +407,8 @@
             s = lax.rem(cx + off, n_ctx)
             arrived(precv.at[kv, s], pr_rcv.at[kv, s])
         over_ctx(sum_wait)
-        total = lax.fori_loop(0, n_ctx, lambda s, t: t + precv[kv, s], jnp.zeros((2, part, HD), F32))
+        total = lax.fori_loop(
+            1, n_ctx, lambda off, t: t + precv[kv, lax.rem(cx + off, n_ctx)].astype(F32), pacc[kv, cx])
         dpk_ref[:, kc] = (total[0] * scale).astype(BF16)
         dpv_ref[:, kc] = total[1].astype(BF16)
 
@@ -395,6 +456,29 @@
     over_ctx(sent)
 
 
+def place_results(*refs):
+    count = (len(refs) - 2) // 3
+    ins, outs, held, (got, put) = refs[:count], refs[count:2 * count], refs[2 * count:-2], refs[-2:]
+    steps = []
+    for i in range(count):
+        pieces = PIECES if i == 0 else 1
+        rows = ins[i].shape[0] // pieces
+        for p in range(pieces):
+            at = pl.ds(p * rows, rows)
+            n = len(steps)
+            steps.append((
+                pltpu.make_async_copy(ins[i].at[at], held[i].at[at], got.at[n]),
+                pltpu.make_async_copy(held[i].at[at], outs[i].at[at], put.at[n]),
+            ))
+    for get, _ in steps:
+        get.start()
+    for get, send in steps:
+        get.wait()
+        send.start()
+    for _, send in steps:
+        send.wait()
+
+
 def shards(n_ctx, n_head, *arrays):
     query_rows, key_rows, _, _, _, log_norm, prefix_keys, _, blocks, members = arrays
     rows, total_width = query_rows.shape
@@ -408,9 +492,8 @@
     slot = -(-own // 8) * 8
     hbm = pl.BlockSpec(memory_space=pl.ANY)
     vmem = pl.BlockSpec(memory_space=pltpu.VMEM)
-    smem = pl.BlockSpec(memory_space=pltpu.SMEM)
     dma = pltpu.SemaphoreType.DMA
-    return pl.pallas_call(
+    results = pl.pallas_call(
         functools.partial(
             kernel, n_ctx=n_ctx, n_head=n_head, nprompt=nprompt, own=own, kvl=kvl),
         out_shape=(
@@ -420,7 +503,7 @@
             jax.ShapeDtypeStruct((part, kvw), BF16),
             jax.ShapeDtypeStruct((part, kvw), BF16),
         ),
-        in_specs=[hbm] * 5 + [vmem] * 3 + [smem] * 2,
+        in_specs=[hbm] * 10,
         out_specs=(hbm, vmem, vmem, vmem, vmem),
         scratch_shapes=[
             pltpu.VMEM((own, tokens, HD), BF16),
@@ -434,12 +517,15 @@
             pltpu.VMEM((HD, ptot + 2 * tokens), BF16),
             pltpu.VMEM((rows, total_width), BF16),
             pltpu.VMEM((rows, total_width), BF16),
+            pltpu.VMEM(log_norm.shape, F32),
+            pltpu.SMEM(blocks.shape, jnp.int32),
+            pltpu.SMEM(members.shape, jnp.int32),
             pltpu.VMEM((n_head, slot, rows), F32),
             pltpu.VMEM((n_head, slot, rows), F32),
             pltpu.VMEM((2 * tokens, tokens), F32),
             pltpu.VMEM((1, tokens), jnp.int32),
             pltpu.SMEM(blocks.shape, jnp.int32),
-            pltpu.VMEM((HD, tokens), F32),
+            pltpu.VMEM((own, HD, tokens), F32),
             pltpu.VMEM((own, tokens, HD), BF16),
             pltpu.VMEM((kvl, tokens, HD), F32),
             pltpu.VMEM((kvl, tokens, HD), F32),
@@ -448,18 +534,27 @@
             pltpu.VMEM((kvl, 2, tokens, HD), BF16),
             pltpu.VMEM((kvl, 2, tokens, HD), BF16),
             pltpu.VMEM((kvl, n_ctx, 2, part, HD), F32),
-            pltpu.VMEM((kvl, n_ctx, 2, part, HD), F32),
+            pltpu.VMEM((kvl, n_ctx, 2, part, HD), BF16),
+            pltpu.VMEM((kvl, n_ctx, 2, part, HD), BF16),
             dma((own, n_head)), dma((own, n_head)), dma((own, n_head)), dma((own, n_head)),
             dma((2, n_head)), dma((2, n_head)), dma((2, n_head)), dma((2, n_head)),
             dma((2, n_ctx)), dma((2, n_ctx)),
             dma((kvl, n_ctx)), dma((kvl, n_ctx)),
             dma((kvl,)), dma((kvl,)),
             dma((n_head,)), dma((n_head,)),
-            dma((4,)), dma((own,)),
+            dma((9,)), dma((own,)),
         ],
         compiler_params=pltpu.CompilerParams(
-            collective_id=0, has_side_effects=True, vmem_limit_bytes=48 * 1024 * 1024),
+            collective_id=0, has_side_effects=True, vmem_limit_bytes=VMEM_BYTES),
     )(*arrays)
+    return pl.pallas_call(
+        place_results,
+        out_shape=tuple(jax.ShapeDtypeStruct(a.shape, a.dtype) for a in results),
+        in_specs=[hbm] * len(results),
+        out_specs=(hbm,) * len(results),
+        scratch_shapes=[pltpu.VMEM(a.shape, a.dtype) for a in results]
+        + [dma((len(results) + PIECES,))] * 2,
+    )(*results)
 
 
 def solution(mesh):

time: 74.4 us -> 60.4 us (0.81)
  local copies, waits for them, and re-layouts: 11.6 us -> 0 us
  Pallas kernels: 61.7 us -> 59.6 us
    unnamed x23 -> x0, local copies, waits for them, and re-layouts: 11.6 us -> none
    pallas_call x1, Pallas kernels: 61.7 us -> 57.2 us  [shards(): pl.pallas_call(functools.partial(kernel, n_ctx=n_ctx, n_head=n_head, npro...]
    pallas_call x0 -> x1, Pallas kernels: none -> 2.36 us  [shards(): pl.pallas_call(place_results, out_shape=tuple((jax.ShapeDtypeStruct(a.sha...]
where the time goes in v2:
time: 60.4 us; the launch traced here: 60.2 us
  Pallas kernels  59.6 us (99%)
  between operations  0.64 us (1%)
    pallas_call x1, Pallas kernels, shards(): pl.pallas_call(functools.partial(kernel, n_ctx=n_ctx, n_head=n_head, npro...  57.2 us
    pallas_call x1, Pallas kernels, shards(): pl.pallas_call(place_results, out_shape=tuple((jax.ShapeDtypeStruct(a.sha...  2.36 us

profile of v2, /device:TPU:0, one launch (start us, length us, event | category | flops | bytes accessed | tf_op | source)
XLA Modules:
  0.0 60.2 jit_solution(1026902876048668438)
XLA Ops:
  0.6 57.2 %shard_map.137 = (bf16[512,1280]{1,0:T(8,128)(2,1)}, bf16[512,256]{1,0:T(8,128)(2,1)}, bf16[512,256]{1,0:T(8,128)(2,1)}, bf16[16,256]{1,0:T(8,128)(2,1)}, bf16[16,256]{1,0:T(8,128)(2,1)}) custom-call(bf16[128,5120]{1,0:T(8,128)(2,1)} %q_hbm.1, bf16[128,1024]{1,0:T(8,128)(2,1)} %k_hbm.1, bf16[128,1024]{1,0:T(8,128)(2,1)} %v_hbm.1, bf16[128,5120]{1,0:T(8,128)(2,1)} %o_hbm.1, ...), custom_call_target="tpu_custom_call" | custom-call | tf_op jit(solution)/shard_map/pallas_call | solution.py:496
  57.9 2.4 %shard_map.138 = (bf16[512,1280]{1,0:T(8,128)(2,1)}, bf16[512,256]{1,0:T(8,128)(2,1)}, bf16[512,256]{1,0:T(8,128)(2,1)}, bf16[16,256]{1,0:T(8,128)(2,1)}, bf16[16,256]{1,0:T(8,128)(2,1)}) custom-call(bf16[512,1280]{1,0:T(8,128)(2,1)} %get-tuple-element.10.refs_0_, bf16[512,256]{1,0:T(8,128)(2,1)} %get-tuple-element.11.refs_1_, ...), custom_call_target="tpu_custom_call" | custom-call | tf_op jit(solution)/shard_map/pallas_call | solution.py:550
